TPU v7x, 32 devices: a whole 2x2x4 slice. The times are simulated.
32 devices in a mesh: dp: 4 (over y, core), seq: 8 (over z, x).
Axes of the slice: x: 2, y: 2, z: 4, core: 2. Of those that a mesh axis runs over, the one named last changes fastest.
Arguments:
- region: bfloat16 [32, 512, 192], P(('dp', 'seq')), parts along dimension 0, may hold values from -11 to 11
- norm_gain: float32 [192], replicated, may hold values from 0.1 to 1.9
- in_weight: bfloat16 [192, 768], replicated, may hold values from -0.4375 to 0.4375
- conv_weight: float32 [9, 384], replicated, may hold values from -2 to 2
- conv_bias: float32 [384], replicated, may hold values from -3 to 3
- coupling_weight: bfloat16 [384, 512], replicated, may hold values from -0.3125 to 0.3125
- step_weight: bfloat16 [384, 24], replicated, may hold values from -0.3125 to 0.3125
- step_bias: float32 [24], replicated, may hold values from -1 to 1
- decay_log: float32 [24], replicated, may hold values from -16 to -2.9
- skip_gain: float32 [24], replicated, may hold values from 0.5 to 12
- out_gain: float32 [384], replicated, may hold values from 0.1 to 1.9
- out_weight: bfloat16 [384, 192], replicated, may hold values from -0.3125 to 0.3125
Outputs:
- refined: bfloat16 [32, 512, 192], P(('dp', 'seq')), parts along dimension 0
There are 4 independent parts, one for each index of `dp`. A program takes and returns all parts, laid end to end along the dimension named above; an argument that names none is the same for every part. Nothing has to cross between parts.
All inputs are finite; a program needn't handle non-finite values.
Results may differ from a plain program's by a relative error of at most 0.0035.
The roundings to bfloat16 on the way count: a program that leaves them out, or rounds other values in their place, can miss the bound.
Values may be sent and summed in bfloat16 or wider, within the bound.
A program may use at most 128 MiB of HBM per device.

v0:
```python
import functools
import jax
import jax.numpy as jnp
from jax import lax
from jax.experimental import pallas as pl
from jax.experimental.pallas import tpu as pltpu
from jax.sharding import PartitionSpec as P

EPSILON = 1e-05
BF = jnp.bfloat16
F32 = jnp.float32
TILE = 128


def mm(a, b):
    return jnp.dot(a, b, preferred_element_type=F32)


def mm_nt(a, b):
    return lax.dot_general(a, b, (((1,), (1,)), ((), ())), preferred_element_type=F32)


def mm_tn(a, b):
    return lax.dot_general(a, b, (((0,), (0,)), ((), ())), preferred_element_type=F32)


def split3(v):
    hi = v.astype(BF)
    rest = v - hi.astype(F32)
    mid = rest.astype(BF)
    lo = (rest - mid.astype(F32)).astype(BF)
    return hi, mid, lo


def iota(shape, dim):
    return lax.broadcasted_iota(jnp.int32, shape, dim)


def kernel(
    n,
    heads,
    state,
    region_ref,
    norm_gain_ref,
    in_w_ref,
    conv_w_ref,
    conv_b_ref,
    coup_w_ref,
    step_w_ref,
    step_b_ref,
    decay_ref,
    skip_ref,
    out_gain_ref,
    out_w_ref,
    out_ref,
    halo,
    pre,
    gate,
    act,
    colbuf,
    xcol,
    xe,
    xo,
    coup,
    cum,
    cum_t,
    step_t,
    own_row,
    own_col,
    msg,
    got,
    tot,
    got_tot,
    ent_out,
    ent_in,
    col_out,
    col_in,
    halo_send,
    halo_recv,
    a_send,
    a_recv,
    s_send,
    s_recv,
    t_send,
    t_recv,
    e_send,
    e_recv,
    c_send,
    c_recv,
):
    me = lax.axis_index("seq")
    tokens, width = region_ref.shape[1], region_ref.shape[2]
    inner = out_w_ref.shape[1]
    band = tokens // n
    head = inner // heads
    part = state // n
    head_bits = head.bit_length() - 1
    n_bits = n.bit_length() - 1
    band_bits = band.bit_length() - 1
    groups = 4 * heads

    def peer_of(k):
        return lax.rem(me + k, n)

    def source_of(k):
        return lax.rem(me + n - k, n)

    barrier = pltpu.get_barrier_semaphore()

    def greet(k, _):
        pl.semaphore_signal(barrier, inc=1, device_id={"seq": peer_of(k)})
        return 0

    lax.fori_loop(1, n, greet, 0)
    pl.semaphore_wait(barrier, n - 1)

    def halo_copy(slot, device):
        return pltpu.make_async_remote_copy(
            src_ref=region_ref.at[0],
            dst_ref=halo.at[slot],
            send_sem=halo_send.at[slot],
            recv_sem=halo_recv.at[slot],
            device_id={"seq": device},
        )

    @pl.when(me < n - 1)
    def _():
        halo_copy(0, me + 1).start()

    @pl.when(me > 0)
    def _():
        halo_copy(1, me - 1).start()

    def normed(values):
        mean_square = jnp.mean(values * values, axis=-1, keepdims=True)
        return (values * lax.rsqrt(mean_square + EPSILON) * norm_gain_ref[...]).astype(BF)

    edge = jnp.zeros((8, inner), F32)
    for a in range(3):
        pre[a, 0:8, :] = edge
        pre[a, tokens + 8 : tokens + 16, :] = edge
    own = mm(normed(region_ref[0].astype(F32)), in_w_ref[...]).astype(BF)
    pre[1, 8 : tokens + 8, :] = own[:, :inner].astype(F32)
    gate[...] = own[:, inner:]

    @pl.when(me < n - 1)
    def _():
        halo_copy(1, me + 1).wait_recv()
        halo_copy(0, me + 1).wait_send()

    @pl.when(me == n - 1)
    def _():
        halo[1] = jnp.zeros((tokens, width), BF)

    @pl.when(me > 0)
    def _():
        halo_copy(0, me - 1).wait_recv()
        halo_copy(1, me - 1).wait_send()

    @pl.when(me == 0)
    def _():
        halo[0] = jnp.zeros((tokens, width), BF)

    for slot, a in ((0, 0), (1, 2)):
        rim = mm(normed(halo[slot].astype(F32)), in_w_ref[:, :inner]).astype(BF)
        pre[a, 8 : tokens + 8, :] = rim.astype(F32)

    per = TILE // band if band < TILE else 1
    for c in range(tokens // TILE):
        summed = conv_b_ref[...]
        for a in range(3):
            for b in range(3):
                first = c * TILE + 7 + b
                tap = 3 * a + b
                summed = summed + pre[a, first : first + TILE, :] * conv_w_ref[tap : tap + 1, :]
        done = (summed / (1.0 + jnp.exp(-summed))).astype(BF)
        if band <= TILE:
            act[c * per : (c + 1) * per] = done.reshape(per, band, inner)
        else:
            where = c * TILE // band
            start = c * TILE % band
            act[where, start : start + TILE] = done

    def a_copy(k, chunk, place):
        return pltpu.make_async_remote_copy(
            src_ref=act.at[chunk],
            dst_ref=colbuf.at[place],
            send_sem=a_send.at[k],
            recv_sem=a_recv.at[k],
            device_id={"seq": chunk},
        )

    def s_copy(p, k, chunk, place):
        return pltpu.make_async_remote_copy(
            src_ref=msg.at[p, chunk],
            dst_ref=got.at[p, place],
            send_sem=s_send.at[p, k],
            recv_sem=s_recv.at[p, k],
            device_id={"seq": chunk},
        )

    def t_copy(p, k, chunk, place):
        return pltpu.make_async_remote_copy(
            src_ref=tot.at[p],
            dst_ref=got_tot.at[p, place],
            send_sem=t_send.at[p, k],
            recv_sem=t_recv.at[p, k],
            device_id={"seq": chunk},
        )

    def e_copy(p, k, chunk, place):
        return pltpu.make_async_remote_copy(
            src_ref=ent_out.at[p, chunk],
            dst_ref=ent_in.at[p, place],
            send_sem=e_send.at[p, k],
            recv_sem=e_recv.at[p, k],
            device_id={"seq": chunk},
        )

    def c_copy(k, chunk, place):
        return pltpu.make_async_remote_copy(
            src_ref=col_out.at[chunk],
            dst_ref=col_in.at[place],
            send_sem=c_send.at[k],
            recv_sem=c_recv.at[k],
            device_id={"seq": chunk},
        )

    def start_all(make):
        def one(k, _):
            make(k, peer_of(k), me).start()
            return 0

        lax.fori_loop(1, n, one, 0)

    def wait_all(make):
        def one(k, _):
            make(k, peer_of(k), source_of(k)).wait_recv()
            return 0

        lax.fori_loop(1, n, one, 0)

    def wait_sent(make):
        def one(k, _):
            make(k, peer_of(k), source_of(k)).wait_send()
            return 0

        lax.fori_loop(1, n, one, 0)

    start_all(a_copy)
    colbuf[pl.ds(me, 1)] = act[pl.ds(me, 1)]

    group_lane = iota((1, groups), 1)
    behind_lane = lax.rem(group_lane, 2 * heads) >= heads
    lower = (iota((tokens, tokens), 0) >= iota((tokens, tokens), 1)).astype(BF)
    eye = (iota((groups, groups), 0) == iota((groups, groups), 1)).astype(BF)
    spread_row = iota((groups, inner), 0)
    spread_head = jnp.right_shift(iota((groups, inner), 1), head_bits)
    rates = -jnp.exp(decay_ref[...])

    def spreader(base):
        return (spread_row == base + spread_head).astype(F32)

    def expand(v, e):
        hi, mid, lo = (piece.astype(F32) for piece in split3(v))
        pieces = jnp.concatenate([hi, mid, lo], axis=1).astype(BF)
        return mm(pieces, jnp.concatenate([e, e, e], axis=0).astype(BF))

    def flip_axes(v):
        hi, mid, lo = split3(v)
        return mm_nt(eye, hi) + mm_nt(eye, mid) + mm_nt(eye, lo)

    def prepare(p, x):
        first = p * 4 * state
        coup[p] = mm(x, coup_w_ref[:, first : first + 4 * state]).astype(BF)
        logits = mm_nt(x, step_w_ref[...]) + step_b_ref[...]
        steps = jnp.maximum(logits, 0.0) + jnp.log1p(jnp.exp(-jnp.abs(logits)))
        logs = rates * steps
        hi, mid, lo = split3(logs)
        ahead = mm(lower, hi) + mm(lower, mid) + mm(lower, lo)
        total = ahead[tokens - 1 : tokens, :]
        c = jnp.where(behind_lane, total - ahead + logs, ahead)
        cum[p] = c
        cum_t[p] = flip_axes(c)
        step_t[p] = flip_axes(steps)
        tail = jnp.exp(total - c) * steps
        base = p * 2 * heads
        xf = x.astype(F32)
        spread_a, spread_b = spreader(base), spreader(base + heads)
        tot[p, :, 0:groups] = jnp.broadcast_to(total, (8, groups))
        start_all(functools.partial(t_copy, p))
        got_tot[p, pl.ds(me, 1)] = tot[p][None]
        contribs = []
        for o, e in ((0, spread_a), (1, spread_b)):
            weighted = (xf * expand(tail, e)).astype(BF)
            writer = coup[p, :, 2 * o * state : (2 * o + 1) * state]
            contribs.append(mm_tn(writer, weighted))
        for d in range(n):
            pieces = [v[d * part : (d + 1) * part] for v in contribs]
            if 2 * part < 16:
                pieces.append(jnp.zeros((16 - 2 * part, inner), F32))
            msg[p, d] = jnp.concatenate(pieces, axis=0).astype(BF)
        start_all(functools.partial(s_copy, p))
        got[p, pl.ds(me, 1)] = msg[p, pl.ds(me, 1)]
        def diagonal(o):
            w = coup[p, :, 2 * o * state : (2 * o + 1) * state].astype(F32)
            r = coup[p, :, (2 * o + 1) * state : (2 * o + 2) * state].astype(F32)
            return jnp.sum(w * r, axis=-1, keepdims=True)

        diag = (jnp.where(behind_lane, diagonal(1), diagonal(0)) * steps).astype(BF).astype(F32)
        target = own_col if p else own_row
        target[...] = xf * expand(diag + skip_ref[...], spread_a + spread_b)
        even = jnp.bitwise_and(iota((1, inner), 1), head) == 0
        xe[...] = jnp.where(even, xf, 0.0).astype(BF)
        xo[...] = jnp.where(even, 0.0, xf).astype(BF)

    def mix(p, first, last):
        target = own_col if p else own_row

        def tile(i, _):
            t0 = pl.multiple_of(i * TILE, TILE)
            rows = pl.ds(t0, TILE)
            both = coup[p, rows, :]
            ahead = mm_nt(both[:, state : 2 * state], coup[p, :, 0:state])
            behind = mm_nt(both[:, 3 * state : 4 * state], coup[p, :, 2 * state : 3 * state])
            t = iota((TILE, tokens), 0) + t0
            s = iota((TILE, tokens), 1)
            after = t > s
            scores = jnp.where(after, ahead, jnp.where(t < s, behind, 0.0))
            c = cum[p, rows, :]

            def weights(h):
                f = p * 2 * heads + h
                g = f + heads
                lead = c[:, f : f + 1] - cum_t[p, f : f + 1, :]
                back = c[:, g : g + 1] - cum_t[p, g : g + 1, :]
                step = jnp.where(after, step_t[p, f : f + 1, :], step_t[p, g : g + 1, :])
                return (scores * jnp.exp(jnp.minimum(lead, back)) * step).astype(BF)

            for j in range(heads // 2):
                lanes = slice(2 * j * head, 2 * (j + 1) * head)
                inside = mm(weights(2 * j), xe[:, lanes]) + mm(weights(2 * j + 1), xo[:, lanes])
                target[rows, lanes] += inside
            return 0

        lax.fori_loop(first, last, tile, 0)

    def scan(p):
        wait_all(functools.partial(t_copy, p))
        base = p * 2 * heads
        totals = jnp.exp(
            jnp.concatenate([got_tot[p, i, 0:8, 0:groups] for i in range(n)], axis=0)
        )
        fade_a = expand(totals, spreader(base))
        fade_b = expand(totals, spreader(base + heads))
        wait_all(functools.partial(s_copy, p))
        entry = jnp.zeros((part, inner), F32)
        ahead = []
        for i in range(n):
            ahead.append(entry)
            entry = fade_a[8 * i : 8 * i + 1] * entry + got[p, i].astype(F32)[0:part]
        entry = jnp.zeros((part, inner), F32)
        for i in reversed(range(n)):
            pieces = [ahead[i], entry]
            if 2 * part < 16:
                pieces.append(jnp.zeros((16 - 2 * part, inner), F32))
            ent_out[p, i] = jnp.concatenate(pieces, axis=0).astype(BF)
            entry = fade_b[8 * i : 8 * i + 1] * entry + got[p, i].astype(F32)[part : 2 * part]
        start_all(functools.partial(e_copy, p))
        ent_in[p, pl.ds(me, 1)] = ent_out[p, pl.ds(me, 1)]

    def finish(p):
        wait_all(functools.partial(e_copy, p))
        target = own_col if p else own_row
        arrived = [ent_in[p, i].astype(F32) for i in range(n)]
        grown = jnp.exp(cum[p])
        base = p * 2 * heads
        result = target[...]
        for o in range(2):
            entry = jnp.concatenate(
                [v[o * part : (o + 1) * part] for v in arrived], axis=0
            ).astype(BF)
            reader = coup[p, :, (2 * o + 1) * state : (2 * o + 2) * state]
            result = result + mm(reader, entry) * expand(grown, spreader(base + o * heads))
        return result

    x_row = act[...].reshape(tokens, inner)
    prepare(0, x_row)
    tiles = tokens // TILE
    mix(0, 0, tiles)
    wait_all(a_copy)
    place = iota((tokens, tokens), 0)
    cell = iota((tokens, tokens), 1)
    turn = cell == jnp.left_shift(jnp.bitwise_and(place, n - 1), band_bits) + jnp.right_shift(place, n_bits)
    xcol[...] = mm(turn.astype(BF), colbuf[...].reshape(tokens, inner)).astype(BF)
    prepare(1, xcol[...])
    scan(0)
    mix(1, 0, tiles // 2)
    scan(1)
    mix(1, tiles // 2, tiles)
    column = finish(1).astype(BF)
    back = cell == jnp.left_shift(jnp.bitwise_and(place, band - 1), n_bits) + jnp.right_shift(place, band_bits)
    col_out[...] = mm(back.astype(BF), column).astype(BF).reshape(n, band, inner)
    start_all(c_copy)
    col_in[pl.ds(me, 1)] = col_out[pl.ds(me, 1)]
    row_total = finish(0)
    g = gate[...].astype(F32)
    own_row[...] = row_total
    own_col[...] = g / (1.0 + jnp.exp(-g))
    wait_all(c_copy)
    for c in range(tokens // TILE):
        rows = slice(c * TILE, (c + 1) * TILE)
        if band <= TILE:
            col = col_in[c * per : (c + 1) * per].reshape(TILE, inner)
        else:
            start = c * TILE % band
            col = col_in[c * TILE // band, start : start + TILE]
        gated = (own_row[rows, :] + col.astype(F32)) * own_col[rows, :]
        mean_square = jnp.mean(gated * gated, axis=-1, keepdims=True)
        normy = (gated * lax.rsqrt(mean_square + EPSILON) * out_gain_ref[...]).astype(BF)
        out_ref[0, rows, :] = (
            region_ref[0, rows, :].astype(F32) + mm_nt(normy, out_w_ref[...])
        ).astype(BF)
    wait_sent(a_copy)
    for p in range(2):
        wait_sent(functools.partial(s_copy, p))
        wait_sent(functools.partial(t_copy, p))
        wait_sent(functools.partial(e_copy, p))
    wait_sent(c_copy)


def body(n, *args):
    region = args[0]
    rows, tokens, width = region.shape
    inner = args[11].shape[0]
    groups = args[7].shape[0]
    heads = groups // 4
    state = args[5].shape[1] // 8
    band = tokens // n
    part = state // n
    flat = [v if v.ndim > 1 else v.reshape(1, -1) for v in args]
    flat[6] = flat[6].T
    flat[11] = flat[11].T
    ent_rows = max(16, 2 * part)
    dma = pltpu.SemaphoreType.DMA
    vmem = pltpu.VMEM
    return pl.pallas_call(
        functools.partial(kernel, n, heads, state),
        out_shape=jax.ShapeDtypeStruct(region.shape, BF),
        in_specs=[pl.BlockSpec(memory_space=pltpu.VMEM)] * len(flat),
        out_specs=pl.BlockSpec(memory_space=pltpu.VMEM),
        scratch_shapes=[
            vmem((2, tokens, width), BF),
            vmem((3, tokens + 16, inner), F32),
            vmem((tokens, inner), BF),
            vmem((n, band, inner), BF),
            vmem((n, band, inner), BF),
            vmem((tokens, inner), BF),
            vmem((tokens, inner), BF),
            vmem((tokens, inner), BF),
            vmem((2, tokens, 4 * state), BF),
            vmem((2, tokens, groups), F32),
            vmem((2, groups, tokens), F32),
            vmem((2, groups, tokens), F32),
            vmem((tokens, inner), F32),
            vmem((tokens, inner), F32),
            vmem((2, n, ent_rows, inner), BF),
            vmem((2, n, ent_rows, inner), BF),
            vmem((2, 8, 128), F32),
            vmem((2, n, 8, 128), F32),
            vmem((2, n, ent_rows, inner), BF),
            vmem((2, n, ent_rows, inner), BF),
            vmem((n, band, inner), BF),
            vmem((n, band, inner), BF),
            dma((2,)),
            dma((2,)),
            dma((n,)),
            dma((n,)),
            dma((2, n)),
            dma((2, n)),
            dma((2, n)),
            dma((2, n)),
            dma((2, n)),
            dma((2, n)),
            dma((n,)),
            dma((n,)),
        ],
        compiler_params=pltpu.CompilerParams(
            collective_id=0, has_side_effects=True, vmem_limit_bytes=50 * 1024 * 1024
        ),
    )(*flat)


def solution(mesh):
    in_specs = (P(("dp", "seq"), None, None),) + (P(),) * 11
    return jax.shard_map(
        functools.partial(body, mesh.shape["seq"]),
        mesh=mesh,
        in_specs=in_specs,
        out_specs=P(("dp", "seq"), None, None),
        check_vma=False,
    )
```

profile of v0, /device:TPU:0, one launch (start us, length us, event | category | flops | bytes accessed | tf_op | source)
XLA Modules:
  0.0 57.8 jit_solution(543481630736624212)
XLA Ops:
  0.0 0.0 copy-start
  0.0 0.7 %reshape.19.conv_b_ref = f32[1,384]{1,0:T(1,128)S(1)} reshape(f32[384]{0:T(512)} %param.16) | data formatting | bytes 3072 | tf_op jit(solution)/shard_map/reshape | solution.py:441
  0.7 0.7 %reshape.23.out_gain_ref = f32[1,384]{1,0:T(1,128)S(1)} reshape(f32[384]{0:T(512)} %param.22) | data formatting | bytes 3072 | tf_op jit(solution)/shard_map/reshape | solution.py:441
  1.4 0.0 copy-start.3
  1.4 0.0 copy-start.4
  1.4 0.0 copy-start.5
  1.4 0.0 copy-start.6
  1.4 0.0 copy-start.7
  1.4 0.0 copy-start.8
  1.5 1.1 %copy.13.region_ref = bf16[1,512,192]{2,1,0:T(8,128)(2,1)S(1)} copy(bf16[1,512,192]{1,2,0:T(8,128)(2,1)} %param.12) | data formatting | bytes 393216 | tf_op args[0]
  2.6 0.0 copy-done
  2.6 0.0 copy-done.3
  2.6 0.0 copy-done.4
  2.6 0.0 copy-done.5
  2.6 0.0 copy-done.6
  2.6 0.0 copy-done.7
  2.6 0.0 copy-done.8
  2.6 0.0 copy-start.1
  2.7 1.0 %copy-done.1 = bf16[192,768]{1,0:T(8,128)(2,1)S(1)} copy-done((bf16[192,768]{1,0:T(8,128)(2,1)S(1)}, bf16[192,768]{1,0:T(8,128)(2,1)}, u32[]{:S(2)}) %copy-start.1) | copy-done | bytes 294936
  3.6 0.0 copy-start.2
  3.6 0.9 %copy-done.2 = bf16[384,192]{0,1:T(8,128)(2,1)S(1)} copy-done((bf16[384,192]{0,1:T(8,128)(2,1)S(1)}, bf16[384,192]{0,1:T(8,128)(2,1)}, u32[]{:S(2)}) %copy-start.2) | copy-done | bytes 147480
  4.5 52.5 %shard_map.118 = bf16[1,512,192]{2,1,0:T(8,128)(2,1)S(1)} custom-call(bf16[1,512,192]{2,1,0:T(8,128)(2,1)S(1)} %copy.13.region_ref, f32[1,192]{1,0:T(1,128)S(1)} %bitcast.8, bf16[192,768]{1,0:T(8,128)(2,1)S(1)} %copy-done.1, f32[9,384]{1,0:T(8,128)S(1)} %copy-done.3, f32[1,384]{1,0:T(1,128)S(1)} %reshape.19.conv_b_ref, bf16[384,512]{1,0:T(8,128)(2,1)S(1)} %copy-done, ...), custom_call_target="tpu_custom_call" | custom-call | tf_op jit(solution)/shard_map/pallas_call | solution.py:447
  57.0 0.8 %copy.14 = bf16[1,512,192]{1,2,0:T(8,128)(2,1)} copy(bf16[1,512,192]{2,1,0:T(8,128)(2,1)S(1)} %shard_map.118) | data formatting | bytes 393216 | tf_op jit(solution)/shard_map/pallas_call | solution.py:447
Async XLA Ops:
  0.0 2.6 %copy-start = (bf16[384,512]{1,0:T(8,128)(2,1)S(1)}, bf16[384,512]{1,0:T(8,128)(2,1)}, u32[]{:S(2)}) copy-start(bf16[384,512]{1,0:T(8,128)(2,1)} %coup_w_ref.1) | copy-start | bytes 1179652
  1.4 1.2 %copy-start.3 = (f32[9,384]{1,0:T(8,128)S(1)}, f32[9,384]{1,0:T(8,128)}, u32[]{:S(2)}) copy-start(f32[9,384]{1,0:T(8,128)} %conv_w_ref.1) | copy-start | bytes 41476
  1.4 1.2 %copy-start.4 = (bf16[384,24]{0,1:T(8,128)(2,1)S(1)}, bf16[384,24]{0,1:T(8,128)(2,1)}, u32[]{:S(2)}) copy-start(bf16[384,24]{0,1:T(8,128)(2,1)} %param.18) | copy-start | bytes 55300
  1.4 1.2 %copy-start.5 = (f32[192]{0:T(256)S(1)}, f32[192]{0:T(256)}, u32[]{:S(2)}) copy-start(f32[192]{0:T(256)} %param.13) | copy-start | bytes 2308
  1.4 1.2 %copy-start.6 = (f32[24]{0:T(128)S(1)}, f32[24]{0:T(128)}, u32[]{:S(2)}) copy-start(f32[24]{0:T(128)} %param.19) | copy-start | bytes 292
  1.4 1.2 %copy-start.7 = (f32[24]{0:T(128)S(1)}, f32[24]{0:T(128)}, u32[]{:S(2)}) copy-start(f32[24]{0:T(128)} %param.20) | copy-start | bytes 292
  1.4 1.2 %copy-start.8 = (f32[24]{0:T(128)S(1)}, f32[24]{0:T(128)}, u32[]{:S(2)}) copy-start(f32[24]{0:T(128)} %param.21) | copy-start | bytes 292
  2.6 1.0 %copy-start.1 = (bf16[192,768]{1,0:T(8,128)(2,1)S(1)}, bf16[192,768]{1,0:T(8,128)(2,1)}, u32[]{:S(2)}) copy-start(bf16[192,768]{1,0:T(8,128)(2,1)} %in_w_ref.1) | copy-start | bytes 884740
  3.6 0.9 %copy-start.2 = (bf16[384,192]{0,1:T(8,128)(2,1)S(1)}, bf16[384,192]{0,1:T(8,128)(2,1)}, u32[]{:S(2)}) copy-start(bf16[384,192]{0,1:T(8,128)(2,1)} %param.23) | copy-start | bytes 442372
where the time goes:
time: 58.4 us; the launch traced here: 57.8 us
  Pallas kernels  52.5 us (90%)
  local copies, waits for them, and re-layouts  5.23 us (9%)
    pallas_call x1, Pallas kernels, body(): pl.pallas_call(functools.partial(kernel, n, heads, state), out_shape=jax....  52.5 us
    unnamed x19, local copies, waits for them, and re-layouts  3.01 us
    reshape x2, local copies, waits for them, and re-layouts, body(): flat = [v if v.ndim > 1 else v.reshape(1, -1) for v in args]  1.42 us

commit v1 on v0

v1 whole, which is shorter than its diff:
```python
import functools
import math
import jax
import jax.numpy as jnp
from jax import lax
from jax.experimental import pallas as pl
from jax.experimental.pallas import tpu as pltpu
from jax.sharding import PartitionSpec as P

EPSILON = 1e-05
BF = jnp.bfloat16
F32 = jnp.float32
TILE = 128
LOG2E = math.log2(math.e)


def mm(a, b):
    return jnp.dot(a, b, preferred_element_type=F32)


def mm_nt(a, b):
    return lax.dot_general(a, b, (((1,), (1,)), ((), ())), preferred_element_type=F32)


def mm_tn(a, b):
    return lax.dot_general(a, b, (((0,), (0,)), ((), ())), preferred_element_type=F32)


def split(v, count):
    pieces = []
    for _ in range(count):
        piece = v.astype(BF).astype(F32)
        pieces.append(piece)
        v = v - piece
    return jnp.concatenate(pieces, axis=0).astype(BF)


def iota(shape, dim):
    return lax.broadcasted_iota(jnp.int32, shape, dim)


def silu(v):
    return v / (1.0 + jnp.exp(-v))


def bits(v):
    return v.bit_length() - 1


def roll_lanes(v, shift):
    shift = shift % v.shape[1]
    return v if shift == 0 else pltpu.roll(v, shift, 1)


def kernel(
    n,
    heads,
    state,
    block,
    region_hbm,
    norm_gain_ref,
    in_w_hbm,
    conv_w_hbm,
    conv_b_ref,
    coup_w_hbm,
    step_w_hbm,
    step_b_ref,
    decay_ref,
    skip_ref,
    out_gain_ref,
    out_w_hbm,
    out_ref,
    region_ref,
    in_w_ref,
    conv_w_ref,
    coup_w_ref,
    step_w_ref,
    out_w_ref,
    cells,
    got_cells,
    halo,
    pre,
    pcol,
    gate,
    xs,
    coup,
    cum,
    step_t,
    contrib,
    fade,
    grown,
    own,
    msg,
    got,
    tot,
    got_tot,
    ent_out,
    ent_in,
    col_out,
    col_in,
    local_sem,
    r_send,
    r_recv,
    halo_send,
    halo_recv,
    s_send,
    s_recv,
    t_send,
    t_recv,
    e_send,
    e_recv,
    c_send,
    c_recv,
):
    me = lax.axis_index("seq")
    width, tokens = region_ref.shape
    inner = out_w_ref.shape[1]
    band = tokens // n
    head = inner // heads
    part = state // n
    groups = 4 * heads
    count = tokens // block
    span = block // n
    fold = TILE // band
    slab = width // fold
    edge_row = slab

    def peer_of(k):
        return lax.rem(me + k, n)

    def source_of(k):
        return lax.rem(me + n - k, n)

    barrier = pltpu.get_barrier_semaphore()

    def greet(k, _):
        pl.semaphore_signal(barrier, inc=1, device_id={"seq": peer_of(k)})
        return 0

    lax.fori_loop(1, n, greet, 0)

    fetch = [
        pltpu.make_async_copy(source, target, local_sem.at[i])
        for i, (source, target) in enumerate(
            (
                (region_hbm.at[0], region_ref),
                (in_w_hbm, in_w_ref),
                (conv_w_hbm, conv_w_ref),
                (coup_w_hbm, coup_w_ref),
                (step_w_hbm, step_w_ref),
                (out_w_hbm, out_w_ref),
            )
        )
    ]
    for copy in fetch:
        copy.start()

    def r_copy(k, chunk, place):
        return pltpu.make_async_remote_copy(
            src_ref=cells.at[chunk],
            dst_ref=got_cells.at[place],
            send_sem=r_send.at[k],
            recv_sem=r_recv.at[k],
            device_id={"seq": chunk},
        )

    def halo_copy(slot, device):
        return pltpu.make_async_remote_copy(
            src_ref=region_ref,
            dst_ref=halo.at[slot],
            send_sem=halo_send.at[slot],
            recv_sem=halo_recv.at[slot],
            device_id={"seq": device},
        )

    def s_copy(p, k, chunk, place):
        return pltpu.make_async_remote_copy(
            src_ref=msg.at[p, chunk],
            dst_ref=got.at[p, place],
            send_sem=s_send.at[p, k],
            recv_sem=s_recv.at[p, k],
            device_id={"seq": chunk},
        )

    def t_copy(p, k, chunk, place):
        return pltpu.make_async_remote_copy(
            src_ref=tot.at[p],
            dst_ref=got_tot.at[p, place],
            send_sem=t_send.at[p, k],
            recv_sem=t_recv.at[p, k],
            device_id={"seq": chunk},
        )

    def e_copy(p, k, chunk, place):
        return pltpu.make_async_remote_copy(
            src_ref=ent_out.at[p, chunk],
            dst_ref=ent_in.at[p, place],
            send_sem=e_send.at[p, k],
            recv_sem=e_recv.at[p, k],
            device_id={"seq": chunk},
        )

    def c_copy(k, chunk, place):
        return pltpu.make_async_remote_copy(
            src_ref=col_out.at[chunk],
            dst_ref=col_in.at[place],
            send_sem=c_send.at[k],
            recv_sem=c_recv.at[k],
            device_id={"seq": chunk},
        )

    def start_all(make):
        def one(k, _):
            make(k, peer_of(k), me).start()
            return 0

        lax.fori_loop(1, n, one, 0)

    def wait_all(make):
        def one(k, _):
            make(k, peer_of(k), source_of(k)).wait_recv()
            return 0

        lax.fori_loop(1, n, one, 0)

    def wait_sent(make):
        def one(k, _):
            make(k, peer_of(k), source_of(k)).wait_send()
            return 0

        lax.fori_loop(1, n, one, 0)

    piece = jnp.right_shift(iota((slab, TILE), 1), bits(band))
    fetch[0].wait()
    rest = cells.shape[1] - slab - 8
    sel_row = iota((8 * n, tokens), 0)
    sel_band = jnp.right_shift(sel_row, 3)
    sel_kind = jnp.bitwise_and(sel_row, 7)
    sel_cell = iota((8 * n, tokens), 1)
    side = jnp.where(
        jnp.bitwise_and(sel_kind, 1) == 0, sel_band * band - 1, sel_band * band + band
    )
    hit = sel_cell == side
    low = jnp.where(hit & (sel_kind < 2), 1.0, 0.0).astype(BF)
    high = jnp.where(hit & (sel_kind >= 2) & (sel_kind < 4), 1.0, 0.0).astype(BF)
    edges = mm_nt(low, region_ref[0:TILE, :]) + mm_nt(high, region_ref[width - TILE : width, :])
    for m in range(tokens // TILE):
        lanes = region_ref[:, m * TILE : (m + 1) * TILE].astype(F32)
        for r in range(fold):
            packed = lanes[0:slab]
            packed = roll_lanes(packed, (0 - r) * band)
            for q in range(1, fold):
                moved = roll_lanes(lanes[q * slab : (q + 1) * slab], (q - r) * band)
                packed = jnp.where(piece == q, moved, packed)
            d = m * fold + r
            parts = [packed, edges[8 * d : 8 * d + 8]]
            if rest:
                parts.append(jnp.zeros((rest, TILE), F32))
            cells[d] = jnp.concatenate(parts, axis=0).astype(BF)

    pl.semaphore_wait(barrier, n - 1)
    start_all(r_copy)
    got_cells[pl.ds(me, 1)] = cells[pl.ds(me, 1)]

    gain_row = norm_gain_ref[...]
    gain_col = jnp.broadcast_to(gain_row, (8, width)).T[:, 0:1]

    def normed(values):
        mean_square = jnp.mean(values * values, axis=0, keepdims=True)
        return (values * lax.rsqrt(mean_square + EPSILON) * gain_col).astype(BF)

    edge = jnp.zeros((8, inner), F32)
    for a in range(3):
        pre[a, 0:8, :] = edge
        pre[a, tokens + 8 : tokens + 16, :] = edge
    blank = jnp.zeros((band + 16, inner), F32)
    pcol[0] = blank
    pcol[n + 1] = blank
    for i in (1, 2, 5):
        fetch[i].wait()
    mine = mm_tn(normed(region_ref[...].astype(F32)), in_w_ref[...]).astype(BF)
    pre[1, 8 : tokens + 8, :] = mine[:, :inner].astype(F32)
    gate[...] = silu(mine[:, inner:].astype(F32))
    for i in (3, 4):
        fetch[i].wait()

    wait_all(r_copy)

    @pl.when(me < n - 1)
    def _():
        halo_copy(0, me + 1).start()

    @pl.when(me > 0)
    def _():
        halo_copy(1, me - 1).start()

    for m in range(tokens // TILE):
        slabs = []
        for q in range(fold):
            packed = None
            for r in range(fold):
                moved = roll_lanes(
                    got_cells[m * fold + r, 0:slab, :].astype(F32), (r - q) * band
                )
                packed = moved if packed is None else jnp.where(piece == r, moved, packed)
            slabs.append(packed)
        values = normed(jnp.concatenate(slabs, axis=0))
        done = mm_tn(values, in_w_ref[:, :inner]).astype(BF).astype(F32)
        for r in range(fold):
            pcol[m * fold + r + 1, 8 : band + 8, :] = done[r * band : (r + 1) * band]
    rims = jnp.concatenate(
        [got_cells[i, edge_row : cells.shape[1], :].astype(F32)[0:8] for i in range(n)], axis=0
    )
    rim_low = rims
    rim_high = jnp.where(
        iota((8 * n, TILE), 1) >= 2 * TILE - width, pltpu.roll(rims, 8 * n - 2, 0), 0.0
    )
    mean_square = (
        jnp.sum(rim_low * rim_low, axis=-1, keepdims=True)
        + jnp.sum(rim_high * rim_high, axis=-1, keepdims=True)
    ) / width
    scale = lax.rsqrt(mean_square + EPSILON)
    rim_pre = mm(
        (rim_low * scale * gain_row[:, 0:TILE]).astype(BF), in_w_ref[0:TILE, :inner]
    ) + mm(
        (rim_high * scale * gain_row[:, width - TILE : width]).astype(BF),
        in_w_ref[width - TILE : width, :inner],
    )
    rim_pre = rim_pre.astype(BF).astype(F32)
    for i in range(n):
        pcol[i + 1, 7:8, :] = rim_pre[8 * i : 8 * i + 1]
        pcol[i + 1, band + 8 : band + 9, :] = rim_pre[8 * i + 1 : 8 * i + 2]
    for i in range(n):
        summed = conv_b_ref[...]
        for a in range(3):
            for b in range(3):
                tap = 3 * a + b
                summed = summed + pcol[i + a, 7 + b : 7 + b + band, :] * conv_w_ref[tap : tap + 1, :]
        done = silu(summed).astype(BF)
        for c in range(count):
            start = c * block + i * span
            xs[1, start : start + span, :] = done[c * span : (c + 1) * span]

    group = iota((groups, 1), 0)
    behind_group = lax.rem(group, 2 * heads) >= heads
    behind_lane = lax.rem(iota((1, groups), 1), 2 * heads) >= heads
    eye = iota((groups, groups), 0) == iota((groups, groups), 1)

    def column_of(row):
        return jnp.sum(jnp.where(eye, row, 0.0), axis=1, keepdims=True)

    def row_of(column):
        return jnp.sum(jnp.where(eye, column, 0.0), axis=0, keepdims=True)

    rates = -jnp.exp(column_of(decay_ref[...]))
    step_b = column_of(step_b_ref[...])
    skips = column_of(skip_ref[...])

    def spreader(p):
        where = jnp.right_shift(iota((groups, 2 * inner), 1), bits(head))
        return (iota((groups, 2 * inner), 0) == where + p * 2 * heads).astype(F32)

    def spread(v, e, pieces):
        many = jnp.concatenate([e] * pieces, axis=0).astype(BF)
        return mm_tn(split(v, pieces), many)

    def position(p, v):
        if p == 0:
            return v
        return jnp.bitwise_and(v, span - 1) * n + jnp.right_shift(v, bits(span))

    def rows_of(c):
        return slice(c * block, (c + 1) * block)

    def prepare(p):
        x = xs[p]
        first = p * 4 * state
        coup[p] = mm(x, coup_w_ref[:, first : first + 4 * state]).astype(BF)
        logits = mm_nt(step_w_ref[...], x) + step_b
        steps = jnp.maximum(logits, 0.0) + jnp.log1p(jnp.exp(-jnp.abs(logits)))
        logs = rates * steps
        step_t[p] = steps
        pieces = split(logs, 3)
        earlier = position(p, iota((block, block), 0)) <= position(p, iota((block, block), 1))
        earlier = jnp.where(earlier, 1.0, 0.0).astype(BF)
        e = spreader(p)
        lane = iota((groups, TILE), 1)
        totals = jnp.zeros((groups, TILE), F32)
        whole = jnp.zeros((groups, 1), F32)
        for c in range(count):
            rows = rows_of(c)
            sums = mm(pieces[:, rows], earlier)
            ahead = sums[0:groups] + sums[groups : 2 * groups] + sums[2 * groups : 3 * groups]
            total = ahead[:, block - 1 : block]
            level = jnp.where(behind_group, total - ahead + logs[:, rows], ahead)
            cum[p, :, rows] = level
            totals = jnp.where(lane == c, total, totals)
            whole = whole + total
            tails = spread(jnp.exp(total - level) * steps[:, rows], e, 2)
            xf = xs[p, rows, :].astype(F32)
            for o in range(2):
                weighted = (xf * tails[:, o * inner : (o + 1) * inner]).astype(BF)
                writer = coup[p, rows, 2 * o * state : (2 * o + 1) * state]
                contrib[p, o, c] = mm_tn(writer, weighted)
        tot[p, :, 0:groups] = jnp.broadcast_to(row_of(whole), (8, groups))
        start_all(functools.partial(t_copy, p))
        got_tot[p, pl.ds(me, 1)] = tot[p][None]
        fade[p] = spread(jnp.exp(totals), e, 3)[0:8]
        sums = [contrib[p, 0, 0], contrib[p, 1, count - 1]]
        for c in range(1, count):
            sums[0] = fade[p, c : c + 1, :inner] * sums[0] + contrib[p, 0, c]
            back = count - 1 - c
            sums[1] = fade[p, back : back + 1, inner:] * sums[1] + contrib[p, 1, back]
        for d in range(n):
            pieces = [v[d * part : (d + 1) * part] for v in sums]
            if 2 * part < 16:
                pieces.append(jnp.zeros((16 - 2 * part, inner), F32))
            msg[p, d] = jnp.concatenate(pieces, axis=0).astype(BF)
        start_all(functools.partial(s_copy, p))
        got[p, pl.ds(me, 1)] = msg[p, pl.ds(me, 1)]

    def local(p):
        e = spreader(p)
        both_sides = e[:, :inner] + e[:, inner:]
        eyes = eye.astype(F32)
        rows_tile = min(block, TILE)
        even = jnp.bitwise_and(iota((1, 2 * head), 1), head) == 0
        for c in range(count):
            rows = rows_of(c)
            level = cum[p, :, rows]
            steps = step_t[p, :, rows]
            grown[p, rows, :] = spread(jnp.exp(level), e, 2)
            scaled = level * LOG2E
            source = scaled - jnp.log(steps) * LOG2E
            target = spread(scaled, eyes, 3)
            xf = xs[p, rows, :].astype(F32)
            pairs = []
            for j in range(heads // 2):
                lanes = xf[:, 2 * j * head : 2 * (j + 1) * head]
                pairs.append(
                    jnp.concatenate(
                        [jnp.where(even, lanes, 0.0), jnp.where(even, 0.0, lanes)], axis=0
                    ).astype(BF)
                )
            diagonals = [jnp.zeros((1, block), F32)] * 2
            for q in range(block // rows_tile):
                t0 = q * rows_tile
                mine = coup[p, c * block + t0 : c * block + t0 + rows_tile, :]
                ahead = mm_nt(mine[:, state : 2 * state], coup[p, rows, 0:state])
                behind = mm_nt(mine[:, 3 * state :], coup[p, rows, 2 * state : 3 * state])
                t = iota((rows_tile, block), 0) + t0
                s = iota((rows_tile, block), 1)
                after = position(p, t) > position(p, s)
                same = t == s
                scores = jnp.where(same, 0.0, jnp.where(after, ahead, behind))
                for o, v in enumerate((ahead, behind)):
                    found = jnp.sum(jnp.where(same, v, 0.0), axis=0, keepdims=True)
                    diagonals[o] = diagonals[o] + found

                def weights(h):
                    f = p * 2 * heads + h
                    g = f + heads
                    lead = target[t0 : t0 + rows_tile, f : f + 1] - source[f : f + 1, :]
                    back = target[t0 : t0 + rows_tile, g : g + 1] - source[g : g + 1, :]
                    return (scores * jnp.exp2(jnp.where(after, lead, back))).astype(BF)

                for j in range(heads // 2):
                    pair = jnp.concatenate([weights(2 * j), weights(2 * j + 1)], axis=1)
                    own[
                        p,
                        c * block + t0 : c * block + t0 + rows_tile,
                        2 * j * head : 2 * (j + 1) * head,
                    ] = mm(pair, pairs[j])
            diag = jnp.where(behind_group, diagonals[1], diagonals[0]) * steps
            diag = diag.astype(BF).astype(F32) + skips
            own[p, rows, :] += xf * spread(diag, both_sides, 2)

    def scan(p):
        wait_all(functools.partial(t_copy, p))
        e = spreader(p)
        logs = jnp.concatenate([got_tot[p, i, :, 0:groups] for i in range(n)], axis=0)
        pieces = split(jnp.exp(logs), 3).reshape(3, 8 * n, groups)
        fades = sum(mm(pieces[i], e.astype(BF)) for i in range(3))
        wait_all(functools.partial(s_copy, p))
        entry = jnp.zeros((part, inner), F32)
        ahead = []
        for i in range(n):
            ahead.append(entry)
            entry = fades[8 * i : 8 * i + 1, :inner] * entry + got[p, i].astype(F32)[0:part]
        entry = jnp.zeros((part, inner), F32)
        for i in reversed(range(n)):
            pieces = [ahead[i], entry]
            if 2 * part < 16:
                pieces.append(jnp.zeros((16 - 2 * part, inner), F32))
            ent_out[p, i] = jnp.concatenate(pieces, axis=0).astype(BF)
            entry = (
                fades[8 * i : 8 * i + 1, inner:] * entry + got[p, i].astype(F32)[part : 2 * part]
            )
        start_all(functools.partial(e_copy, p))
        ent_in[p, pl.ds(me, 1)] = ent_out[p, pl.ds(me, 1)]

    def finish(p):
        wait_all(functools.partial(e_copy, p))
        arrived = [ent_in[p, i].astype(F32) for i in range(n)]
        entries = [[None] * count, [None] * count]
        for o in range(2):
            entry = jnp.concatenate([v[o * part : (o + 1) * part] for v in arrived], axis=0)
            order = range(count) if o == 0 else reversed(range(count))
            for c in order:
                entries[o][c] = entry.astype(BF)
                lanes = slice(o * inner, (o + 1) * inner)
                entry = fade[p, c : c + 1, lanes] * entry + contrib[p, o, c]
        for c in range(count):
            rows = rows_of(c)
            result = own[p, rows, :]
            for o in range(2):
                reader = coup[p, rows, (2 * o + 1) * state : (2 * o + 2) * state]
                carried = mm(reader, entries[o][c])
                result = result + carried * grown[p, rows, o * inner : (o + 1) * inner]
            if p == 0:
                own[p, rows, :] = result
            else:
                result = result.astype(BF)
                for i in range(n):
                    col_out[i, c * span : (c + 1) * span, :] = result[i * span : (i + 1) * span]

    prepare(1)
    local(1)
    scan(1)

    @pl.when(me < n - 1)
    def _():
        halo_copy(1, me + 1).wait_recv()
        halo_copy(0, me + 1).wait_send()

    @pl.when(me == n - 1)
    def _():
        halo[1] = jnp.zeros((width, tokens), BF)

    @pl.when(me > 0)
    def _():
        halo_copy(0, me - 1).wait_recv()
        halo_copy(1, me - 1).wait_send()

    @pl.when(me == 0)
    def _():
        halo[0] = jnp.zeros((width, tokens), BF)

    for slot, a in ((0, 0), (1, 2)):
        rim = mm_tn(normed(halo[slot].astype(F32)), in_w_ref[:, :inner]).astype(BF)
        pre[a, 8 : tokens + 8, :] = rim.astype(F32)
    for c in range(tokens // TILE):
        summed = conv_b_ref[...]
        for a in range(3):
            for b in range(3):
                first = c * TILE + 7 + b
                tap = 3 * a + b
                summed = summed + pre[a, first : first + TILE, :] * conv_w_ref[tap : tap + 1, :]
        xs[0, c * TILE : (c + 1) * TILE, :] = silu(summed).astype(BF)
    prepare(0)
    finish(1)
    start_all(c_copy)
    col_in[pl.ds(me, 1)] = col_out[pl.ds(me, 1)]
    local(0)
    scan(0)
    finish(0)
    wait_all(c_copy)
    for c in range(tokens // TILE):
        rows = slice(c * TILE, (c + 1) * TILE)
        per = TILE // band
        col = col_in[c * per : (c + 1) * per].astype(F32).reshape(TILE, inner)
        gated = (own[0, rows, :] + col) * gate[rows, :]
        mean_square = jnp.mean(gated * gated, axis=-1, keepdims=True)
        normy = (gated * lax.rsqrt(mean_square + EPSILON) * out_gain_ref[...]).astype(BF)
        out_ref[0, :, rows] = (
            region_ref[:, rows].astype(F32) + mm_nt(out_w_ref[...], normy)
        ).astype(BF)
    wait_sent(r_copy)
    for p in range(2):
        wait_sent(functools.partial(s_copy, p))
        wait_sent(functools.partial(t_copy, p))
        wait_sent(functools.partial(e_copy, p))
    wait_sent(c_copy)


def body(n, *args):
    region = args[0]
    _, tokens, width = region.shape
    inner = args[11].shape[0]
    groups = args[7].shape[0]
    heads = groups // 4
    state = args[5].shape[1] // 8
    band = tokens // n
    part = state // n
    block = max(TILE, 16 * n)
    count = tokens // block
    fold = TILE // band
    cell_rows = (width // fold + 8 + 15) // 16 * 16
    flat = [v if v.ndim > 1 else v.reshape(1, -1) for v in args]
    flat[0] = jnp.swapaxes(region, 1, 2)
    flat[6] = flat[6].T
    flat[11] = flat[11].T
    ent_rows = max(16, 2 * part)
    dma = pltpu.SemaphoreType.DMA
    vmem = pltpu.VMEM
    in_hbm = (0, 2, 3, 5, 6, 11)
    out = pl.pallas_call(
        functools.partial(kernel, n, heads, state, block),
        out_shape=jax.ShapeDtypeStruct(flat[0].shape, BF),
        in_specs=[
            pl.BlockSpec(memory_space=pl.ANY if i in in_hbm else pltpu.VMEM)
            for i in range(len(flat))
        ],
        out_specs=pl.BlockSpec(memory_space=pltpu.VMEM),
        scratch_shapes=[
            vmem((width, tokens), BF),
            *[vmem(flat[i].shape, flat[i].dtype) for i in in_hbm[1:]],
            vmem((n, cell_rows, TILE), BF),
            vmem((n, cell_rows, TILE), BF),
            vmem((2, width, tokens), BF),
            vmem((3, tokens + 16, inner), F32),
            vmem((n + 2, band + 16, inner), F32),
            vmem((tokens, inner), F32),
            vmem((2, tokens, inner), BF),
            vmem((2, tokens, 4 * state), BF),
            vmem((2, groups, tokens), F32),
            vmem((2, groups, tokens), F32),
            vmem((2, 2, count, state, inner), F32),
            vmem((2, 8, 2 * inner), F32),
            vmem((2, tokens, 2 * inner), F32),
            vmem((2, tokens, inner), F32),
            vmem((2, n, ent_rows, inner), BF),
            vmem((2, n, ent_rows, inner), BF),
            vmem((2, 8, 128), F32),
            vmem((2, n, 8, 128), F32),
            vmem((2, n, ent_rows, inner), BF),
            vmem((2, n, ent_rows, inner), BF),
            vmem((n, band, inner), BF),
            vmem((n, band, inner), BF),
            dma((6,)),
            dma((n,)),
            dma((n,)),
            dma((2,)),
            dma((2,)),
            dma((2, n)),
            dma((2, n)),
            dma((2, n)),
            dma((2, n)),
            dma((2, n)),
            dma((2, n)),
            dma((n,)),
            dma((n,)),
        ],
        compiler_params=pltpu.CompilerParams(
            collective_id=0, has_side_effects=True, vmem_limit_bytes=56 * 1024 * 1024
        ),
    )(*flat)
    return jnp.swapaxes(out, 1, 2)


def solution(mesh):
    in_specs = (P(("dp", "seq"), None, None),) + (P(),) * 11
    return jax.shard_map(
        functools.partial(body, mesh.shape["seq"]),
        mesh=mesh,
        in_specs=in_specs,
        out_specs=P(("dp", "seq"), None, None),
        check_vma=False,
    )
```

time: 58.4 us -> 48.4 us (0.83)
  Pallas kernels: 52.5 us -> 44.6 us
  local copies, waits for them, and re-layouts: 5.23 us -> 3.54 us
    pallas_call x1, Pallas kernels: 52.5 us -> 44.6 us  [body(): pl.pallas_call(functools.partial(kernel, n, heads, state, block), out_sha...]
    pallas_call x1 -> x0, local copies, waits for them, and re-layouts: 0.8 us -> none  [body(): pl.pallas_call(functools.partial(kernel, n, heads, state), out_shape=jax....]
    unnamed x19 -> x5, local copies, waits for them, and re-layouts: 3.01 us -> 2.42 us
where the time goes in v1:
time: 48.4 us; the launch traced here: 48.1 us
  Pallas kernels  44.6 us (92%)
  local copies, waits for them, and re-layouts  3.54 us (7%)
    pallas_call x1, Pallas kernels, body(): pl.pallas_call(functools.partial(kernel, n, heads, state, block), out_sha...  44.6 us
    unnamed x5, local copies, waits for them, and re-layouts  2.42 us
    reshape x2, local copies, waits for them, and re-layouts, body(): flat = [v if v.ndim > 1 else v.reshape(1, -1) for v in args]  1.13 us

profile of v1, /device:TPU:0, one launch (start us, length us, event | category | flops | bytes accessed | tf_op | source)
XLA Modules:
  0.0 48.1 jit_solution(14740382284566106925)
XLA Ops:
  0.0 0.0 copy-start
  0.0 0.7 %copy-done = f32[384]{0:T(512)S(1)} copy-done((f32[384]{0:T(512)S(1)}, f32[384]{0:T(512)}, u32[]{:S(2)}) %copy-start) | copy-done | bytes 1560
  0.7 0.0 copy-start.1
  0.7 0.6 %reshape.19.conv_b_ref = f32[1,384]{1,0:T(1,128)} reshape(f32[384]{0:T(512)S(1)} %copy-done) | data formatting | bytes 3072 | tf_op jit(solution)/shard_map/reshape | solution.py:599
  1.2 0.1 copy-done.1
  1.4 0.6 %reshape.23.out_gain_ref = f32[1,384]{1,0:T(1,128)} reshape(f32[384]{0:T(512)S(1)} %copy-done.1) | data formatting | bytes 3072 | tf_op jit(solution)/shard_map/reshape | solution.py:599
  1.9 44.6 %shard_map.118 = bf16[1,192,512]{2,1,0:T(8,128)(2,1)} custom-call(bf16[1,192,512]{2,1,0:T(8,128)(2,1)} %bitcast.9, f32[1,192]{1,0:T(1,128)} %bitcast.12, bf16[192,768]{1,0:T(8,128)(2,1)} %in_w_hbm.1, f32[9,384]{1,0:T(8,128)} %conv_w_hbm.1, f32[1,384]{1,0:T(1,128)} %reshape.19.conv_b_ref, bf16[384,512]{1,0:T(8,128)(2,1)} %coup_w_hbm.1, ...), custom_call_target="tpu_custom_call" | custom-call | tf_op jit(solution)/shard_map/pallas_call | solution.py:607
  46.5 1.6 %copy.14 = bf16[1,512,192]{1,2,0:T(8,128)(2,1)} copy(bf16[1,512,192]{1,2,0:T(8,128)(2,1)} %bitcast.8) | data formatting | bytes 393216
Async XLA Ops:
  0.0 0.7 %copy-start = (f32[384]{0:T(512)S(1)}, f32[384]{0:T(512)}, u32[]{:S(2)}) copy-start(f32[384]{0:T(512)} %param.16) | copy-start | bytes 4612
  0.7 0.7 %copy-start.1 = (f32[384]{0:T(512)S(1)}, f32[384]{0:T(512)}, u32[]{:S(2)}) copy-start(f32[384]{0:T(512)} %param.22) | copy-start | bytes 4612

commit v2 on v1

--- a/solution.py
+++ b/solution.py
@@ -40,11 +40,29 @@
 
 
 def silu(v):
-    return v / (1.0 + jnp.exp(-v))
+    half = 0.5 * v
+    return half * jnp.tanh(half) + half
+
+
+def depthwise(planes, weights, bias, size):
+    sums = []
+    for b in range(3):
+        total = planes[0] * weights[b : b + 1, :]
+        for a in (1, 2):
+            tap = 3 * a + b
+            total = total + planes[a] * weights[tap : tap + 1, :]
+        sums.append(total)
+    rows = sums[0].shape[0]
+    moved = pltpu.roll(sums[0], 1, 0) + pltpu.roll(sums[2], rows - 1, 0)
+    return silu((sums[1] + moved)[8 : 8 + size] + bias)
 
 
 def bits(v):
     return v.bit_length() - 1
+
+
+def one_row(ref):
+    return jnp.concatenate([ref[i : i + 1, :] for i in range(ref.shape[0])], axis=1)
 
 
 def roll_lanes(v, shift):
@@ -92,8 +110,6 @@
     own,
     msg,
     got,
-    tot,
-    got_tot,
     ent_out,
     ent_in,
     col_out,
@@ -105,8 +121,6 @@
     halo_recv,
     s_send,
     s_recv,
-    t_send,
-    t_recv,
     e_send,
     e_recv,
     c_send,
@@ -179,15 +193,6 @@
             dst_ref=got.at[p, place],
             send_sem=s_send.at[p, k],
             recv_sem=s_recv.at[p, k],
-            device_id={"seq": chunk},
-        )
-
-    def t_copy(p, k, chunk, place):
-        return pltpu.make_async_remote_copy(
-            src_ref=tot.at[p],
-            dst_ref=got_tot.at[p, place],
-            send_sem=t_send.at[p, k],
-            recv_sem=t_recv.at[p, k],
             device_id={"seq": chunk},
         )
 
@@ -260,9 +265,20 @@
 
     pl.semaphore_wait(barrier, n - 1)
     start_all(r_copy)
+
+    @pl.when(me < n - 1)
+    def _():
+        halo_copy(0, me + 1).start()
+
+    @pl.when(me > 0)
+    def _():
+        halo_copy(1, me - 1).start()
+
     got_cells[pl.ds(me, 1)] = cells[pl.ds(me, 1)]
 
     gain_row = norm_gain_ref[...]
+    conv_b = one_row(conv_b_ref)
+    out_gain = one_row(out_gain_ref)
     gain_col = jnp.broadcast_to(gain_row, (8, width)).T[:, 0:1]
 
     def normed(values):
@@ -285,14 +301,6 @@
         fetch[i].wait()
 
     wait_all(r_copy)
-
-    @pl.when(me < n - 1)
-    def _():
-        halo_copy(0, me + 1).start()
-
-    @pl.when(me > 0)
-    def _():
-        halo_copy(1, me - 1).start()
 
     for m in range(tokens // TILE):
         slabs = []
@@ -331,12 +339,8 @@
         pcol[i + 1, 7:8, :] = rim_pre[8 * i : 8 * i + 1]
         pcol[i + 1, band + 8 : band + 9, :] = rim_pre[8 * i + 1 : 8 * i + 2]
     for i in range(n):
-        summed = conv_b_ref[...]
-        for a in range(3):
-            for b in range(3):
-                tap = 3 * a + b
-                summed = summed + pcol[i + a, 7 + b : 7 + b + band, :] * conv_w_ref[tap : tap + 1, :]
-        done = silu(summed).astype(BF)
+        planes = [pcol[i + a] for a in range(3)]
+        done = depthwise(planes, conv_w_ref, conv_b, band).astype(BF)
         for c in range(count):
             start = c * block + i * span
             xs[1, start : start + span, :] = done[c * span : (c + 1) * span]
@@ -350,7 +354,8 @@
         return jnp.sum(jnp.where(eye, row, 0.0), axis=1, keepdims=True)
 
     def row_of(column):
-        return jnp.sum(jnp.where(eye, column, 0.0), axis=0, keepdims=True)
+        here = iota((groups, TILE), 0) == iota((groups, TILE), 1)
+        return jnp.sum(jnp.where(here, column, 0.0), axis=0, keepdims=True)
 
     rates = -jnp.exp(column_of(decay_ref[...]))
     step_b = column_of(step_b_ref[...])
@@ -402,9 +407,14 @@
                 weighted = (xf * tails[:, o * inner : (o + 1) * inner]).astype(BF)
                 writer = coup[p, rows, 2 * o * state : (2 * o + 1) * state]
                 contrib[p, o, c] = mm_tn(writer, weighted)
-        tot[p, :, 0:groups] = jnp.broadcast_to(row_of(whole), (8, groups))
-        start_all(functools.partial(t_copy, p))
-        got_tot[p, pl.ds(me, 1)] = tot[p][None]
+        left = row_of(whole)
+        line = iota((msg.shape[2], TILE), 0)
+        totals_sent = jnp.zeros((msg.shape[2], TILE), F32)
+        for i in range(3):
+            rounded = left.astype(BF).astype(F32)
+            totals_sent = jnp.where(line == i, rounded, totals_sent)
+            left = left - rounded
+        totals_sent = totals_sent.astype(BF)
         fade[p] = spread(jnp.exp(totals), e, 3)[0:8]
         sums = [contrib[p, 0, 0], contrib[p, 1, count - 1]]
         for c in range(1, count):
@@ -415,7 +425,8 @@
             pieces = [v[d * part : (d + 1) * part] for v in sums]
             if 2 * part < 16:
                 pieces.append(jnp.zeros((16 - 2 * part, inner), F32))
-            msg[p, d] = jnp.concatenate(pieces, axis=0).astype(BF)
+            msg[p, d, :, 0:inner] = jnp.concatenate(pieces, axis=0).astype(BF)
+            msg[p, d, :, inner:] = totals_sent
         start_all(functools.partial(s_copy, p))
         got[p, pl.ds(me, 1)] = msg[p, pl.ds(me, 1)]
 
@@ -476,17 +487,19 @@
             own[p, rows, :] += xf * spread(diag, both_sides, 2)
 
     def scan(p):
-        wait_all(functools.partial(t_copy, p))
+        wait_all(functools.partial(s_copy, p))
         e = spreader(p)
-        logs = jnp.concatenate([got_tot[p, i, :, 0:groups] for i in range(n)], axis=0)
-        pieces = split(jnp.exp(logs), 3).reshape(3, 8 * n, groups)
+        logs = jnp.concatenate(
+            [got[p, i, :, inner:].astype(F32)[0:8] for i in range(n)], axis=0
+        )
+        logs = logs + pltpu.roll(logs, 8 * n - 1, 0) + pltpu.roll(logs, 8 * n - 2, 0)
+        pieces = split(jnp.exp(logs[:, 0:groups]), 3).reshape(3, 8 * n, groups)
         fades = sum(mm(pieces[i], e.astype(BF)) for i in range(3))
-        wait_all(functools.partial(s_copy, p))
         entry = jnp.zeros((part, inner), F32)
         ahead = []
         for i in range(n):
             ahead.append(entry)
-            entry = fades[8 * i : 8 * i + 1, :inner] * entry + got[p, i].astype(F32)[0:part]
+            entry = fades[8 * i : 8 * i + 1, :inner] * entry + got[p, i, :, 0:inner].astype(F32)[0:part]
         entry = jnp.zeros((part, inner), F32)
         for i in reversed(range(n)):
             pieces = [ahead[i], entry]
@@ -494,7 +507,7 @@
                 pieces.append(jnp.zeros((16 - 2 * part, inner), F32))
             ent_out[p, i] = jnp.concatenate(pieces, axis=0).astype(BF)
             entry = (
-                fades[8 * i : 8 * i + 1, inner:] * entry + got[p, i].astype(F32)[part : 2 * part]
+                fades[8 * i : 8 * i + 1, inner:] * entry + got[p, i, :, 0:inner].astype(F32)[part : 2 * part]
             )
         start_all(functools.partial(e_copy, p))
         ent_in[p, pl.ds(me, 1)] = ent_out[p, pl.ds(me, 1)]
@@ -525,9 +538,6 @@
                     col_out[i, c * span : (c + 1) * span, :] = result[i * span : (i + 1) * span]
 
     prepare(1)
-    local(1)
-    scan(1)
-
     @pl.when(me < n - 1)
     def _():
         halo_copy(1, me + 1).wait_recv()
@@ -550,19 +560,17 @@
         rim = mm_tn(normed(halo[slot].astype(F32)), in_w_ref[:, :inner]).astype(BF)
         pre[a, 8 : tokens + 8, :] = rim.astype(F32)
     for c in range(tokens // TILE):
-        summed = conv_b_ref[...]
-        for a in range(3):
-            for b in range(3):
-                first = c * TILE + 7 + b
-                tap = 3 * a + b
-                summed = summed + pre[a, first : first + TILE, :] * conv_w_ref[tap : tap + 1, :]
-        xs[0, c * TILE : (c + 1) * TILE, :] = silu(summed).astype(BF)
+        planes = [pre[a, c * TILE : (c + 1) * TILE + 16, :] for a in range(3)]
+        done = depthwise(planes, conv_w_ref, conv_b, TILE)
+        xs[0, c * TILE : (c + 1) * TILE, :] = done.astype(BF)
     prepare(0)
+    local(1)
+    scan(1)
+    local(0)
+    scan(0)
     finish(1)
     start_all(c_copy)
     col_in[pl.ds(me, 1)] = col_out[pl.ds(me, 1)]
-    local(0)
-    scan(0)
     finish(0)
     wait_all(c_copy)
     for c in range(tokens // TILE):
@@ -571,14 +579,13 @@
         col = col_in[c * per : (c + 1) * per].astype(F32).reshape(TILE, inner)
         gated = (own[0, rows, :] + col) * gate[rows, :]
         mean_square = jnp.mean(gated * gated, axis=-1, keepdims=True)
-        normy = (gated * lax.rsqrt(mean_square + EPSILON) * out_gain_ref[...]).astype(BF)
+        normy = (gated * lax.rsqrt(mean_square + EPSILON) * out_gain).astype(BF)
         out_ref[0, :, rows] = (
             region_ref[:, rows].astype(F32) + mm_nt(out_w_ref[...], normy)
         ).astype(BF)
     wait_sent(r_copy)
     for p in range(2):
         wait_sent(functools.partial(s_copy, p))
-        wait_sent(functools.partial(t_copy, p))
         wait_sent(functools.partial(e_copy, p))
     wait_sent(c_copy)
 
@@ -597,6 +604,9 @@
     fold = TILE // band
     cell_rows = (width // fold + 8 + 15) // 16 * 16
     flat = [v if v.ndim > 1 else v.reshape(1, -1) for v in args]
+    for i in (4, 10):
+        if args[i].shape[0] % TILE == 0:
+            flat[i] = args[i].reshape(-1, TILE)
     flat[0] = jnp.swapaxes(region, 1, 2)
     flat[6] = flat[6].T
     flat[11] = flat[11].T
@@ -608,7 +618,7 @@
         functools.partial(kernel, n, heads, state, block),
         out_shape=jax.ShapeDtypeStruct(flat[0].shape, BF),
         in_specs=[
-            pl.BlockSpec(memory_space=pl.ANY if i in in_hbm else pltpu.VMEM)
+            pl.BlockSpec(memory_space=pltpu.HBM if i in in_hbm else pltpu.VMEM)
             for i in range(len(flat))
         ],
         out_specs=pl.BlockSpec(memory_space=pltpu.VMEM),
@@ -629,10 +639,8 @@
             vmem((2, 8, 2 * inner), F32),
             vmem((2, tokens, 2 * inner), F32),
             vmem((2, tokens, inner), F32),
-            vmem((2, n, ent_rows, inner), BF),
-            vmem((2, n, ent_rows, inner), BF),
-            vmem((2, 8, 128), F32),
-            vmem((2, n, 8, 128), F32),
+            vmem((2, n, ent_rows, inner + TILE), BF),
+            vmem((2, n, ent_rows, inner + TILE), BF),
             vmem((2, n, ent_rows, inner), BF),
             vmem((2, n, ent_rows, inner), BF),
             vmem((n, band, inner), BF),
@@ -646,13 +654,11 @@
             dma((2, n)),
             dma((2, n)),
             dma((2, n)),
-            dma((2, n)),
-            dma((2, n)),
             dma((n,)),
             dma((n,)),
         ],
         compiler_params=pltpu.CompilerParams(
-            collective_id=0, has_side_effects=True, vmem_limit_bytes=56 * 1024 * 1024
+            collective_id=0, has_side_effects=True, vmem_limit_bytes=57 * 1024 * 1024
         ),
     )(*flat)
     return jnp.swapaxes(out, 1, 2)

time: 48.4 us -> 42.7 us (0.88)
  Pallas kernels: 44.6 us -> 40.9 us
  local copies, waits for them, and re-layouts: 3.54 us -> 1.62 us
    pallas_call x1, Pallas kernels: 44.6 us -> 40.9 us  [body(): pl.pallas_call(functools.partial(kernel, n, heads, state, block), out_sha...]
    reshape x2 -> x0, local copies, waits for them, and re-layouts: 1.13 us -> none  [body(): flat = [v if v.ndim > 1 else v.reshape(1, -1) for v in args]]
    unnamed x5 -> x1, local copies, waits for them, and re-layouts: 2.42 us -> 1.62 us
where the time goes in v2:
time: 42.7 us; the launch traced here: 42.5 us
  Pallas kernels  40.9 us (96%)
  local copies, waits for them, and re-layouts  1.62 us (4%)
    pallas_call x1, Pallas kernels, body(): pl.pallas_call(functools.partial(kernel, n, heads, state, block), out_sha...  40.9 us
    unnamed x1, local copies, waits for them, and re-layouts  1.62 us

profile of v2, /device:TPU:0, one launch (start us, length us, event | category | flops | bytes accessed | tf_op | source)
XLA Modules:
  0.0 42.5 jit_solution(6221682103004081447)
XLA Ops:
  0.0 40.9 %shard_map.118 = bf16[1,192,512]{2,1,0:T(8,128)(2,1)} custom-call(bf16[1,192,512]{2,1,0:T(8,128)(2,1)} %bitcast.11, f32[1,192]{1,0:T(1,128)} %bitcast.16, bf16[192,768]{1,0:T(8,128)(2,1)} %in_w_hbm.1, f32[9,384]{1,0:T(8,128)} %conv_w_hbm.1, f32[3,128]{1,0:T(4,128)} %bitcast.14, bf16[384,512]{1,0:T(8,128)(2,1)} %coup_w_hbm.1, bf16[24,384]{1,0:T(8,128)(2,1)} %bitcast.13, ...), custom_call_target="tpu_custom_call" | custom-call | tf_op jit(solution)/shard_map/pallas_call | solution.py:617
  40.9 1.6 %copy.14 = bf16[1,512,192]{1,2,0:T(8,128)(2,1)} copy(bf16[1,512,192]{1,2,0:T(8,128)(2,1)} %bitcast.10) | data formatting | bytes 393216

commit v3 on v2

--- a/solution.py
+++ b/solution.py
@@ -76,23 +76,29 @@
     state,
     block,
     region_hbm,
-    norm_gain_ref,
+    norm_gain_hbm,
     in_w_hbm,
     conv_w_hbm,
-    conv_b_ref,
+    conv_b_hbm,
     coup_w_hbm,
     step_w_hbm,
+    step_b_hbm,
+    decay_hbm,
+    skip_hbm,
+    out_gain_hbm,
+    out_w_hbm,
+    out_ref,
+    region_ref,
+    norm_gain_ref,
+    in_w_ref,
+    conv_w_ref,
+    conv_b_ref,
+    coup_w_ref,
+    step_w_ref,
     step_b_ref,
     decay_ref,
     skip_ref,
     out_gain_ref,
-    out_w_hbm,
-    out_ref,
-    region_ref,
-    in_w_ref,
-    conv_w_ref,
-    coup_w_ref,
-    step_w_ref,
     out_w_ref,
     cells,
     got_cells,
@@ -139,32 +145,44 @@
     slab = width // fold
     edge_row = slab
 
-    def peer_of(k):
-        return lax.rem(me + k, n)
-
-    def source_of(k):
-        return lax.rem(me + n - k, n)
+    ring = [(k, lax.rem(me + k, n), lax.rem(me + n - k, n)) for k in range(1, n)]
 
     barrier = pltpu.get_barrier_semaphore()
 
-    def greet(k, _):
-        pl.semaphore_signal(barrier, inc=1, device_id={"seq": peer_of(k)})
-        return 0
-
-    lax.fori_loop(1, n, greet, 0)
-
+    for _, peer, _ in ring:
+        pl.semaphore_signal(barrier, inc=1, device_id={"seq": peer})
+
+    sources = (
+        region_hbm.at[0],
+        norm_gain_hbm,
+        in_w_hbm,
+        conv_w_hbm,
+        conv_b_hbm,
+        coup_w_hbm,
+        step_w_hbm,
+        step_b_hbm,
+        decay_hbm,
+        skip_hbm,
+        out_gain_hbm,
+        out_w_hbm,
+    )
+    targets = (
+        region_ref,
+        norm_gain_ref,
+        in_w_ref,
+        conv_w_ref,
+        conv_b_ref,
+        coup_w_ref,
+        step_w_ref,
+        step_b_ref,
+        decay_ref,
+        skip_ref,
+        out_gain_ref,
+        out_w_ref,
+    )
     fetch = [
         pltpu.make_async_copy(source, target, local_sem.at[i])
-        for i, (source, target) in enumerate(
-            (
-                (region_hbm.at[0], region_ref),
-                (in_w_hbm, in_w_ref),
-                (conv_w_hbm, conv_w_ref),
-                (coup_w_hbm, coup_w_ref),
-                (step_w_hbm, step_w_ref),
-                (out_w_hbm, out_w_ref),
-            )
-        )
+        for i, (source, target) in enumerate(zip(sources, targets))
     ]
     for copy in fetch:
         copy.start()
@@ -214,26 +232,17 @@
             device_id={"seq": chunk},
         )
 
-    def start_all(make):
-        def one(k, _):
-            make(k, peer_of(k), me).start()
-            return 0
-
-        lax.fori_loop(1, n, one, 0)
-
-    def wait_all(make):
-        def one(k, _):
-            make(k, peer_of(k), source_of(k)).wait_recv()
-            return 0
-
-        lax.fori_loop(1, n, one, 0)
-
-    def wait_sent(make):
-        def one(k, _):
-            make(k, peer_of(k), source_of(k)).wait_send()
-            return 0
-
-        lax.fori_loop(1, n, one, 0)
+    def start_all(make, partners=ring):
+        for k, peer, _ in partners:
+            make(k, peer, me).start()
+
+    def wait_all(make, partners=ring):
+        for k, peer, source in partners:
+            make(k, peer, source).wait_recv()
+
+    def wait_sent(make, partners=ring):
+        for k, peer, source in partners:
+            make(k, peer, source).wait_send()
 
     piece = jnp.right_shift(iota((slab, TILE), 1), bits(band))
     fetch[0].wait()
@@ -276,6 +285,8 @@
 
     got_cells[pl.ds(me, 1)] = cells[pl.ds(me, 1)]
 
+    for copy in fetch[1:]:
+        copy.wait()
     gain_row = norm_gain_ref[...]
     conv_b = one_row(conv_b_ref)
     out_gain = one_row(out_gain_ref)
@@ -292,13 +303,9 @@
     blank = jnp.zeros((band + 16, inner), F32)
     pcol[0] = blank
     pcol[n + 1] = blank
-    for i in (1, 2, 5):
-        fetch[i].wait()
     mine = mm_tn(normed(region_ref[...].astype(F32)), in_w_ref[...]).astype(BF)
     pre[1, 8 : tokens + 8, :] = mine[:, :inner].astype(F32)
     gate[...] = silu(mine[:, inner:].astype(F32))
-    for i in (3, 4):
-        fetch[i].wait()
 
     wait_all(r_copy)
 
@@ -564,13 +571,13 @@
         done = depthwise(planes, conv_w_ref, conv_b, TILE)
         xs[0, c * TILE : (c + 1) * TILE, :] = done.astype(BF)
     prepare(0)
+    scan(1)
     local(1)
-    scan(1)
-    local(0)
     scan(0)
     finish(1)
     start_all(c_copy)
     col_in[pl.ds(me, 1)] = col_out[pl.ds(me, 1)]
+    local(0)
     finish(0)
     wait_all(c_copy)
     for c in range(tokens // TILE):
@@ -613,18 +620,15 @@
     ent_rows = max(16, 2 * part)
     dma = pltpu.SemaphoreType.DMA
     vmem = pltpu.VMEM
-    in_hbm = (0, 2, 3, 5, 6, 11)
+    flat = [pltpu.with_memory_space_constraint(v, pltpu.HBM) for v in flat]
     out = pl.pallas_call(
         functools.partial(kernel, n, heads, state, block),
         out_shape=jax.ShapeDtypeStruct(flat[0].shape, BF),
-        in_specs=[
-            pl.BlockSpec(memory_space=pltpu.HBM if i in in_hbm else pltpu.VMEM)
-            for i in range(len(flat))
-        ],
+        in_specs=[pl.BlockSpec(memory_space=pltpu.HBM)] * len(flat),
         out_specs=pl.BlockSpec(memory_space=pltpu.VMEM),
         scratch_shapes=[
             vmem((width, tokens), BF),
-            *[vmem(flat[i].shape, flat[i].dtype) for i in in_hbm[1:]],
+            *[vmem(v.shape, v.dtype) for v in flat[1:]],
             vmem((n, cell_rows, TILE), BF),
             vmem((n, cell_rows, TILE), BF),
             vmem((2, width, tokens), BF),
@@ -645,7 +649,7 @@
             vmem((2, n, ent_rows, inner), BF),
             vmem((n, band, inner), BF),
             vmem((n, band, inner), BF),
-            dma((6,)),
+            dma((len(flat),)),
             dma((n,)),
             dma((n,)),
             dma((2,)),
@@ -658,7 +662,7 @@
             dma((n,)),
         ],
         compiler_params=pltpu.CompilerParams(
-            collective_id=0, has_side_effects=True, vmem_limit_bytes=57 * 1024 * 1024
+            collective_id=0, has_side_effects=True, vmem_limit_bytes=40 * 1024 * 1024
         ),
     )(*flat)
     return jnp.swapaxes(out, 1, 2)

time: 42.7 us -> 39.6 us (0.927)
  Pallas kernels: 40.9 us -> 38.7 us
  local copies, waits for them, and re-layouts: 1.62 us -> 0.68 us
    pallas_call x1, Pallas kernels: 40.9 us -> 38.7 us  [body(): pl.pallas_call(functools.partial(kernel, n, heads, state, block), out_sha...]
    unnamed x1, local copies, waits for them, and re-layouts: 1.62 us -> 0.68 us
where the time goes in v3:
time: 39.6 us; the launch traced here: 39.4 us
  Pallas kernels  38.7 us (98%)
  local copies, waits for them, and re-layouts  0.68 us (2%)
    pallas_call x1, Pallas kernels, body(): pl.pallas_call(functools.partial(kernel, n, heads, state, block), out_sha...  38.7 us

profile of v3, /device:TPU:0, one launch (start us, length us, event | category | flops | bytes accessed | tf_op | source)
XLA Modules:
  0.0 39.4 jit_solution(12059321062500816588)
XLA Ops:
  0.0 38.7 %shard_map.118 = bf16[1,192,512]{2,1,0:T(8,128)(2,1)S(1)} custom-call(bf16[1,192,512]{2,1,0:T(8,128)(2,1)} %bitcast.11, f32[1,192]{1,0:T(1,128)} %bitcast.16, bf16[192,768]{1,0:T(8,128)(2,1)} %in_w_hbm.1, f32[9,384]{1,0:T(8,128)} %conv_w_hbm.1, f32[3,128]{1,0:T(4,128)} %bitcast.14, bf16[384,512]{1,0:T(8,128)(2,1)} %coup_w_hbm.1, bf16[24,384]{1,0:T(8,128)(2,1)} %bitcast.13, ...), custom_call_target="tpu_custom_call" | custom-call | tf_op jit(solution)/shard_map/pallas_call | solution.py:624
  38.8 0.7 %copy.14 = bf16[1,512,192]{1,2,0:T(8,128)(2,1)} copy(bf16[1,512,192]{1,2,0:T(8,128)(2,1)S(1)} %bitcast.10) | data formatting | bytes 393216

commit v4 on v3

--- a/solution.py
+++ b/solution.py
@@ -44,17 +44,22 @@
     return half * jnp.tanh(half) + half
 
 
-def depthwise(planes, weights, bias, size):
-    sums = []
-    for b in range(3):
-        total = planes[0] * weights[b : b + 1, :]
-        for a in (1, 2):
-            tap = 3 * a + b
-            total = total + planes[a] * weights[tap : tap + 1, :]
-        sums.append(total)
-    rows = sums[0].shape[0]
-    moved = pltpu.roll(sums[0], 1, 0) + pltpu.roll(sums[2], rows - 1, 0)
-    return silu((sums[1] + moved)[8 : 8 + size] + bias)
+def depthwise(load, weights, bias, size):
+    parts = []
+    for q in range(weights.shape[1] // TILE):
+        lanes = slice(q * TILE, (q + 1) * TILE)
+        planes = [load(a, lanes) for a in range(3)]
+        sums = []
+        for b, first, last in ((0, 0, size + 8), (1, 8, size + 8), (2, 8, size + 16)):
+            total = planes[0][first:last] * weights[b : b + 1, lanes]
+            for a in (1, 2):
+                tap = 3 * a + b
+                total = total + planes[a][first:last] * weights[tap : tap + 1, lanes]
+            sums.append(total)
+        left = pltpu.roll(sums[0], 1, 0)[8:]
+        right = pltpu.roll(sums[2], size + 7, 0)[:size]
+        parts.append(silu(sums[1] + bias[:, lanes] + (left + right)))
+    return jnp.concatenate(parts, axis=1)
 
 
 def bits(v):
@@ -346,8 +351,7 @@
         pcol[i + 1, 7:8, :] = rim_pre[8 * i : 8 * i + 1]
         pcol[i + 1, band + 8 : band + 9, :] = rim_pre[8 * i + 1 : 8 * i + 2]
     for i in range(n):
-        planes = [pcol[i + a] for a in range(3)]
-        done = depthwise(planes, conv_w_ref, conv_b, band).astype(BF)
+        done = depthwise(lambda a, lanes: pcol[i + a, :, lanes], conv_w_ref, conv_b, band).astype(BF)
         for c in range(count):
             start = c * block + i * span
             xs[1, start : start + span, :] = done[c * span : (c + 1) * span]
@@ -567,8 +571,8 @@
         rim = mm_tn(normed(halo[slot].astype(F32)), in_w_ref[:, :inner]).astype(BF)
         pre[a, 8 : tokens + 8, :] = rim.astype(F32)
     for c in range(tokens // TILE):
-        planes = [pre[a, c * TILE : (c + 1) * TILE + 16, :] for a in range(3)]
-        done = depthwise(planes, conv_w_ref, conv_b, TILE)
+        span_rows = slice(c * TILE, (c + 1) * TILE + 16)
+        done = depthwise(lambda a, lanes: pre[a, span_rows, lanes], conv_w_ref, conv_b, TILE)
         xs[0, c * TILE : (c + 1) * TILE, :] = done.astype(BF)
     prepare(0)
     scan(1)

time: 39.6 us -> 39 us (0.985)
  Pallas kernels: 38.7 us -> 38.1 us
    pallas_call x1, Pallas kernels: 38.7 us -> 38.1 us  [body(): pl.pallas_call(functools.partial(kernel, n, heads, state, block), out_sha...]
where the time goes in v4:
time: 39 us; the launch traced here: 38.8 us
  Pallas kernels  38.1 us (98%)
  local copies, waits for them, and re-layouts  0.68 us (2%)
    pallas_call x1, Pallas kernels, body(): pl.pallas_call(functools.partial(kernel, n, heads, state, block), out_sha...  38.1 us

profile of v4, /device:TPU:0, one launch (start us, length us, event | category | flops | bytes accessed | tf_op | source)
XLA Modules:
  0.0 38.8 jit_solution(5397234257990041983)
XLA Ops:
  0.0 38.1 %shard_map.118 = bf16[1,192,512]{2,1,0:T(8,128)(2,1)S(1)} custom-call(bf16[1,192,512]{2,1,0:T(8,128)(2,1)} %bitcast.11, f32[1,192]{1,0:T(1,128)} %bitcast.16, bf16[192,768]{1,0:T(8,128)(2,1)} %in_w_hbm.1, f32[9,384]{1,0:T(8,128)} %conv_w_hbm.1, f32[3,128]{1,0:T(4,128)} %bitcast.14, bf16[384,512]{1,0:T(8,128)(2,1)} %coup_w_hbm.1, bf16[24,384]{1,0:T(8,128)(2,1)} %bitcast.13, ...), custom_call_target="tpu_custom_call" | custom-call | tf_op jit(solution)/shard_map/pallas_call | solution.py:628
  38.1 0.7 %copy.14 = bf16[1,512,192]{1,2,0:T(8,128)(2,1)} copy(bf16[1,512,192]{1,2,0:T(8,128)(2,1)S(1)} %bitcast.10) | data formatting | bytes 393216

commit v5 on v4

--- a/solution.py
+++ b/solution.py
@@ -441,6 +441,67 @@
         start_all(functools.partial(s_copy, p))
         got[p, pl.ds(me, 1)] = msg[p, pl.ds(me, 1)]
 
+    def prepare_stacked(p):
+        x = xs[p]
+        first = p * 4 * state
+        coup[p] = mm(x, coup_w_ref[:, first : first + 4 * state]).astype(BF)
+        logits = mm_nt(step_w_ref[...], x) + step_b
+        steps = jnp.maximum(logits, 0.0) + jnp.log1p(jnp.exp(-jnp.abs(logits)))
+        logs = rates * steps
+        step_t[p] = steps
+        earlier = position(p, iota((block, block), 0)) <= position(p, iota((block, block), 1))
+        earlier = jnp.where(earlier, 1.0, 0.0).astype(BF)
+
+        def stack(v):
+            return jnp.concatenate([v[:, rows_of(c)] for c in range(count)], axis=0)
+
+        deep = count * groups
+        behind_deep = lax.rem(iota((deep, 1), 0), 2 * heads) >= heads
+        stacked = stack(logs)
+        sums = mm(split(stacked, 3), earlier)
+        ahead = sums[0:deep] + sums[deep : 2 * deep] + sums[2 * deep : 3 * deep]
+        total = ahead[:, block - 1 : block]
+        level = jnp.where(behind_deep, total - ahead + stacked, ahead)
+        tail = jnp.exp(total - level) * stack(steps)
+        e = spreader(p)
+        lane = iota((groups, TILE), 1)
+        totals = jnp.zeros((groups, TILE), F32)
+        whole = jnp.zeros((groups, 1), F32)
+        for c in range(count):
+            rows = rows_of(c)
+            these = slice(c * groups, (c + 1) * groups)
+            cum[p, :, rows] = level[these]
+            totals = jnp.where(lane == c, total[these], totals)
+            whole = whole + total[these]
+            tails = spread(tail[these], e, 2)
+            xf = xs[p, rows, :].astype(F32)
+            for o in range(2):
+                weighted = (xf * tails[:, o * inner : (o + 1) * inner]).astype(BF)
+                writer = coup[p, rows, 2 * o * state : (2 * o + 1) * state]
+                contrib[p, o, c] = mm_tn(writer, weighted)
+        left = row_of(whole)
+        line = iota((msg.shape[2], TILE), 0)
+        totals_sent = jnp.zeros((msg.shape[2], TILE), F32)
+        for i in range(3):
+            rounded = left.astype(BF).astype(F32)
+            totals_sent = jnp.where(line == i, rounded, totals_sent)
+            left = left - rounded
+        totals_sent = totals_sent.astype(BF)
+        fade[p] = spread(jnp.exp(totals), e, 3)[0:8]
+        sums = [contrib[p, 0, 0], contrib[p, 1, count - 1]]
+        for c in range(1, count):
+            sums[0] = fade[p, c : c + 1, :inner] * sums[0] + contrib[p, 0, c]
+            back = count - 1 - c
+            sums[1] = fade[p, back : back + 1, inner:] * sums[1] + contrib[p, 1, back]
+        for d in range(n):
+            pieces = [v[d * part : (d + 1) * part] for v in sums]
+            if 2 * part < 16:
+                pieces.append(jnp.zeros((16 - 2 * part, inner), F32))
+            msg[p, d, :, 0:inner] = jnp.concatenate(pieces, axis=0).astype(BF)
+            msg[p, d, :, inner:] = totals_sent
+        start_all(functools.partial(s_copy, p))
+        got[p, pl.ds(me, 1)] = msg[p, pl.ds(me, 1)]
+
     def local(p):
         e = spreader(p)
         both_sides = e[:, :inner] + e[:, inner:]
@@ -574,7 +635,7 @@
         span_rows = slice(c * TILE, (c + 1) * TILE + 16)
         done = depthwise(lambda a, lanes: pre[a, span_rows, lanes], conv_w_ref, conv_b, TILE)
         xs[0, c * TILE : (c + 1) * TILE, :] = done.astype(BF)
-    prepare(0)
+    prepare_stacked(0)
     scan(1)
     local(1)
     scan(0)

time: 39 us -> 38.2 us (0.979)
  Pallas kernels: 38.1 us -> 37.3 us
    pallas_call x1, Pallas kernels: 38.1 us -> 37.3 us  [body(): pl.pallas_call(functools.partial(kernel, n, heads, state, block), out_sha...]
where the time goes in v5:
time: 38.2 us; the launch traced here: 38 us
  Pallas kernels  37.3 us (98%)
  local copies, waits for them, and re-layouts  0.68 us (2%)
    pallas_call x1, Pallas kernels, body(): pl.pallas_call(functools.partial(kernel, n, heads, state, block), out_sha...  37.3 us

profile of v5, /device:TPU:0, one launch (start us, length us, event | category | flops | bytes accessed | tf_op | source)
XLA Modules:
  0.0 38.0 jit_solution(5682805276945888233)
XLA Ops:
  0.0 37.3 %shard_map.118 = bf16[1,192,512]{2,1,0:T(8,128)(2,1)S(1)} custom-call(bf16[1,192,512]{2,1,0:T(8,128)(2,1)} %bitcast.11, f32[1,192]{1,0:T(1,128)} %bitcast.16, bf16[192,768]{1,0:T(8,128)(2,1)} %in_w_hbm.1, f32[9,384]{1,0:T(8,128)} %conv_w_hbm.1, f32[3,128]{1,0:T(4,128)} %bitcast.14, bf16[384,512]{1,0:T(8,128)(2,1)} %coup_w_hbm.1, bf16[24,384]{1,0:T(8,128)(2,1)} %bitcast.13, ...), custom_call_target="tpu_custom_call" | custom-call | tf_op jit(solution)/shard_map/pallas_call | solution.py:689
  37.3 0.7 %copy.14 = bf16[1,512,192]{1,2,0:T(8,128)(2,1)} copy(bf16[1,512,192]{1,2,0:T(8,128)(2,1)S(1)} %bitcast.10) | data formatting | bytes 393216

commit v6 on v5

--- a/solution.py
+++ b/solution.py
@@ -644,7 +644,12 @@
     col_in[pl.ds(me, 1)] = col_out[pl.ds(me, 1)]
     local(0)
     finish(0)
+    wait_sent(r_copy)
+    for p in range(2):
+        wait_sent(functools.partial(s_copy, p))
+        wait_sent(functools.partial(e_copy, p))
     wait_all(c_copy)
+    wait_sent(c_copy)
     for c in range(tokens // TILE):
         rows = slice(c * TILE, (c + 1) * TILE)
         per = TILE // band
@@ -655,11 +660,6 @@
         out_ref[0, :, rows] = (
             region_ref[:, rows].astype(F32) + mm_nt(out_w_ref[...], normy)
         ).astype(BF)
-    wait_sent(r_copy)
-    for p in range(2):
-        wait_sent(functools.partial(s_copy, p))
-        wait_sent(functools.partial(e_copy, p))
-    wait_sent(c_copy)
 
 
 def body(n, *args):

time: 38.2 us -> 38.1 us (level)
  no operation moved by 1% of the time
where the time goes in v6:
time: 38.1 us; the launch traced here: 38 us
  Pallas kernels  37.3 us (98%)
  local copies, waits for them, and re-layouts  0.68 us (2%)
    pallas_call x1, Pallas kernels, body(): pl.pallas_call(functools.partial(kernel, n, heads, state, block), out_sha...  37.3 us

profile of v6, /device:TPU:0, one launch (start us, length us, event | category | flops | bytes accessed | tf_op | source)
XLA Modules:
  0.0 38.0 jit_solution(15390821305545979401)
XLA Ops:
  0.0 37.3 %shard_map.118 = bf16[1,192,512]{2,1,0:T(8,128)(2,1)S(1)} custom-call(bf16[1,192,512]{2,1,0:T(8,128)(2,1)} %bitcast.11, f32[1,192]{1,0:T(1,128)} %bitcast.16, bf16[192,768]{1,0:T(8,128)(2,1)} %in_w_hbm.1, f32[9,384]{1,0:T(8,128)} %conv_w_hbm.1, f32[3,128]{1,0:T(4,128)} %bitcast.14, bf16[384,512]{1,0:T(8,128)(2,1)} %coup_w_hbm.1, bf16[24,384]{1,0:T(8,128)(2,1)} %bitcast.13, ...), custom_call_target="tpu_custom_call" | custom-call | tf_op jit(solution)/shard_map/pallas_call | solution.py:689
  37.3 0.7 %copy.14 = bf16[1,512,192]{1,2,0:T(8,128)(2,1)} copy(bf16[1,512,192]{1,2,0:T(8,128)(2,1)S(1)} %bitcast.10) | data formatting | bytes 393216
